TPU v7x, 32 devices: a whole 2x2x4 slice. The times are simulated.
32 devices in a mesh: dp: 2 (over x), ctx: 4 (over y, core), tensor: 4 (over z).
Axes of the slice: x: 2, y: 2, z: 4, core: 2. Of those that a mesh axis runs over, the one named last changes fastest.
Arguments:
- queries: bfloat16 [1024, 3072], P(('dp', 'ctx'), 'tensor'), parts along dimension 0, may hold values from -6 to 6
- keys: bfloat16 [1024, 512], P(('dp', 'ctx'), 'tensor'), parts along dimension 0, may hold values from -6 to 6
- values: bfloat16 [1024, 512], P(('dp', 'ctx'), 'tensor'), parts along dimension 0, may hold values from -6 to 6
- cache_keys: bfloat16 [1024, 512], P(('dp', 'ctx'), 'tensor'), parts along dimension 0, may hold values from -6 to 6
- cache_values: bfloat16 [1024, 512], P(('dp', 'ctx'), 'tensor'), parts along dimension 0, may hold values from -6 to 6
- residual: bfloat16 [1024, 3072], P(('dp', 'ctx'), 'tensor'), parts along dimension 0, may hold values from -36 to 36
- norm_gain: float32 [3072], replicated, may hold values from 0.1 to 1.9
- w_gate: bfloat16 [3072, 65536], P(None, ('ctx', 'tensor')), may hold values from -0.109375 to 0.109375
- w_up: bfloat16 [3072, 65536], P(None, ('ctx', 'tensor')), may hold values from -0.109375 to 0.109375
- w_down: bfloat16 [65536, 3072], P(('ctx', 'tensor')), may hold values from -0.0625 to 0.0625
- expert_ids: int32 [1024, 2], P(('dp', 'ctx')), parts along dimension 0, may hold values from 0 to 7, all different within a row; in each aligned block of 128 rows (0 to 127, 128 to 255, ...) at most 36 rows name the same one
- gate_weights: float32 [1024, 2], P(('dp', 'ctx')), parts along dimension 0, may hold values from 0.1 to 0.9
Outputs:
- layer_out: bfloat16 [1024, 3072], P(('dp', 'ctx'), 'tensor'), parts along dimension 0
There are 2 independent parts, one for each index of `dp`. A program takes and returns all parts, laid end to end along the dimension named above; an argument that names none is the same for every part. Nothing has to cross between parts.
Inputs may be any that keep to these rules, and one draw needn't show every extreme that they name: `expert_ids`: among the 128 rows of each index of ctx (aligned blocks of rows), no expert is named by more than 36 rows, a bound that some block reaches.
All inputs are finite; a program needn't handle non-finite values.
Results may differ from a plain program's by a relative error of at most 0.012.
Values may be sent and summed in bfloat16 or wider, within the bound.
A program may use at most 192 MiB of HBM per device.

v0:
```python
import math

import jax
import jax.numpy as jnp
from jax import lax
from jax.sharding import PartitionSpec as P

HEADS = 24
KV_HEADS = 4
HEAD_DIM = 128
EXPERTS = 8
TOP = 2
CAP = 36


eps = 1e-05
neg_big = -1e30


def attend_block(
    carried, query_heads, key_block, value_block, key_pos, query_pos, window, score_scale
):
    run_max, run_sum, accumulated = carried
    scores = (
        jnp.einsum("qkgd,tkd->kgqt", query_heads, key_block, preferred_element_type=jnp.float32)
        * score_scale
    )
    allowed = (key_pos[None, :] <= query_pos[:, None]) & (
        key_pos[None, :] > query_pos[:, None] - window
    )
    scores = jnp.where(allowed[None, None], scores, neg_big)
    new_max = jnp.maximum(run_max, jnp.max(scores, axis=-1))
    weights = jnp.where(allowed[None, None], jnp.exp(scores - new_max[..., None]), 0.0)
    run_sum = jnp.sum(weights, axis=-1)
    update = jnp.einsum(
        "kgqt,tkd->kgqd",
        weights.astype(jnp.bfloat16),
        value_block,
        preferred_element_type=jnp.float32,
    )
    accumulated = update
    return (new_max, run_sum, accumulated)


def expert_block(full_rows, norm_gain, w_gate, w_up, w_down):
    widened = full_rows.astype(jnp.float32)
    inverse = lax.rsqrt(jnp.mean(widened * widened, axis=-1, keepdims=True) + eps)
    normed = (widened * inverse * norm_gain).astype(jnp.bfloat16)
    gate_proj = jnp.dot(normed, w_gate, preferred_element_type=jnp.float32)
    up_proj = jnp.dot(normed, w_up, preferred_element_type=jnp.float32)
    activated = (jax.nn.silu(gate_proj) * up_proj).astype(jnp.bfloat16)
    return jnp.dot(activated, w_down, preferred_element_type=jnp.float32)


def route_tables(expert_ids, gate_weights):
    tok_rows = expert_ids.shape[0]
    flat_ids = expert_ids.reshape(-1)
    member = (flat_ids[:, None] == jnp.arange(EXPERTS, dtype=jnp.int32)[None, :]).astype(jnp.int32)
    earlier = jnp.cumsum(member, axis=0) - member
    rank_in = jnp.sum(earlier * member, axis=1)
    slot_of = flat_ids * CAP + rank_in
    picks = (jnp.arange(EXPERTS * CAP, dtype=jnp.int32)[:, None] == slot_of[None, :]).astype(
        jnp.float32
    )
    select = jnp.sum(picks.reshape(EXPERTS * CAP, tok_rows, TOP), axis=2).astype(jnp.bfloat16)
    weighing = jnp.sum(
        (picks * gate_weights.reshape(-1)[None, :]).reshape(EXPERTS * CAP, tok_rows, TOP), axis=2
    )
    return (select, weighing)


def per_device(
    queries,
    keys,
    values,
    cache_keys,
    cache_values,
    residual,
    norm_gain,
    w_gate,
    w_up,
    w_down,
    expert_ids,
    gate_weights,
):
    tok_rows = queries.shape[0]
    n_ctx = lax.axis_size("ctx")
    n_tensor = lax.axis_size("tensor")
    window = tok_rows * n_ctx
    kv_local = keys.shape[1] // HEAD_DIM
    group_size = HEADS // KV_HEADS
    score_scale = 1.0 / math.sqrt(HEAD_DIM)
    query_heads = queries.reshape(tok_rows, kv_local, group_size, HEAD_DIM)
    my_index = lax.axis_index("ctx")
    query_pos = my_index * tok_rows + jnp.arange(tok_rows, dtype=jnp.int32)
    initial = (
        jnp.full((kv_local, group_size, tok_rows), neg_big, jnp.float32),
        jnp.zeros((kv_local, group_size, tok_rows), jnp.float32),
        jnp.zeros((kv_local, group_size, tok_rows, HEAD_DIM), jnp.float32),
    )
    stacked = jnp.stack((cache_keys, cache_values, keys, values))
    shard_piece = lax.all_gather(stacked, "ctx", axis=1, tiled=True)
    span_rows = shard_piece.shape[1]
    offsets = jnp.arange(span_rows, dtype=jnp.int32)
    key_block = jnp.concatenate((shard_piece[0], shard_piece[2]), axis=0).reshape(
        2 * span_rows, kv_local, HEAD_DIM
    )
    value_block = jnp.concatenate((shard_piece[1], shard_piece[3]), axis=0).reshape(
        2 * span_rows, kv_local, HEAD_DIM
    )
    key_pos = jnp.concatenate((offsets - window, offsets))
    run_max, run_sum, accumulated = attend_block(
        initial, query_heads, key_block, value_block, key_pos, query_pos, window, score_scale
    )
    attended = (
        (accumulated / run_sum[..., None])
        .transpose(2, 0, 1, 3)
        .reshape(tok_rows, kv_local * group_size * HEAD_DIM)
    )
    hidden_state = (residual.astype(jnp.float32) + attended).astype(jnp.bfloat16)
    select, weighing = route_tables(expert_ids, gate_weights)
    quarter = hidden_state.shape[1]
    buffer = (
        jnp.dot(select, hidden_state, preferred_element_type=jnp.float32)
        .astype(jnp.bfloat16)
        .reshape(EXPERTS, CAP, quarter)
    )
    per_expert = n_ctx * n_tensor // EXPERTS
    outgoing = jnp.repeat(buffer, per_expert, axis=0)
    arrived = lax.all_to_all(outgoing, ("ctx", "tensor"), split_axis=0, concat_axis=2, tiled=True)
    item_count = arrived.shape[1]
    full_rows = arrived.reshape(item_count * n_ctx, n_tensor * quarter)
    partial_value = expert_block(full_rows, norm_gain, w_gate, w_up, w_down)
    gathered_parts = lax.all_to_all(
        partial_value.reshape(item_count, n_ctx * n_tensor, quarter).astype(jnp.bfloat16),
        ("ctx", "tensor"),
        split_axis=1,
        concat_axis=1,
        tiled=True,
    ).astype(jnp.float32)
    expert_out = (
        jnp.sum(gathered_parts.reshape(CAP, EXPERTS, per_expert, quarter), axis=2)
        .transpose(1, 0, 2)
        .reshape(EXPERTS * CAP, quarter)
    )
    mixture = lax.dot_general(
        weighing,
        expert_out,
        (((0,), (0,)), ((), ())),
        precision=lax.Precision.HIGHEST,
        preferred_element_type=jnp.float32,
    )
    return (hidden_state.astype(jnp.float32) + mixture).astype(jnp.bfloat16)


def solution(mesh):
    in_specs = (
        P(("dp", "ctx"), "tensor"),
        P(("dp", "ctx"), "tensor"),
        P(("dp", "ctx"), "tensor"),
        P(("dp", "ctx"), "tensor"),
        P(("dp", "ctx"), "tensor"),
        P(("dp", "ctx"), "tensor"),
        P(),
        P(None, ("ctx", "tensor")),
        P(None, ("ctx", "tensor")),
        P(("ctx", "tensor"), None),
        P(("dp", "ctx"), None),
        P(("dp", "ctx"), None),
    )
    out_specs = P(("dp", "ctx"), "tensor")
    return jax.shard_map(
        per_device, mesh=mesh, in_specs=in_specs, out_specs=out_specs, check_vma=False
    )
```

profile of v0, /device:TPU:0, one launch (start us, length us, event | category | flops | bytes accessed | tf_op | source)
XLA Modules:
  0.0 114.7 jit_solution(16762922204314185309)
XLA Ops:
  0.0 0.8 copy.79
  1.1 0.6 reduce-window.6
  1.7 0.2 slice_reduce_fusion
  2.2 0.7 multiply_add_fusion
  3.0 1.1 copy.74
  4.0 0.8 pad_maximum_fusion
  4.9 8.6 %all_gather.3 = bf16[4,512,128]{2,1,0:T(8,128)(2,1)S(1)} all-gather(bf16[4,128,128]{2,1,0:T(8,128)(2,1)S(1)} %pad_maximum_fusion), channel_id=1, replica_groups=mesh['dp'=2,'ctx'=4,'tensor'=4] {'ctx'}, dimensions={1}, use_global_device_ids=true | all-gather | bytes 655360 | tf_op jit(solution)/shard_map/all_gather | solution.py:102
  13.6 0.2 compare_and_fusion
  13.8 0.6 fusion.1
  14.4 0.8 fusion.7
  15.2 0.9 fusion.16
  16.4 0.8 convert_reduce_fusion.1
  17.1 0.3 convolution_convert_fusion.1
  17.6 30.9 %all_to_all.14 = bf16[16,36,768]{2,1,0:T(8,128)(2,1)S(1)} all-to-all(bf16[16,36,768]{2,1,0:T(8,128)(2,1)S(1)} %bitcast.77), channel_id=1, replica_groups=mesh['dp'=2,'ctx'=4,'tensor'=4] {'ctx','tensor'}, dimensions={0} | all-to-all | bytes 1769472 | tf_op jit(solution)/shard_map/all_to_all | solution.py:130
  48.5 0.3 fusion.9
  49.2 0.6 copy.82
  49.8 0.5 reshape.195
  50.3 13.4 %fusion.34 = f32[144,4096]{1,0:T(8,128)} fusion(bf16[3072,4096]{1,0:T(8,128)(2,1)} %param.19, f32[144,3072]{1,0:T(8,128)S(1)} %reshape.195, f32[3072]{0:T(1024)S(1)} %copy-done.5, f32[144]{0:T(256)S(1)} %add_rsqrt_fusion), kind=kOutput, calls=%fused_computation.64 | convolution fusion | flops 3625205760 | bytes 29307456 | tf_op jit(solution)/shard_map/dot_general | solution.py:49
  63.7 19.5 %convolution_convert_fusion = bf16[144,3072]{1,0:T(8,128)(2,1)S(1)} fusion(bf16[4096,3072]{1,0:T(8,128)(2,1)} %param.21, bf16[3072,4096]{1,0:T(8,128)(2,1)} %param.20, f32[144,4096]{1,0:T(8,128)} %fusion.34, f32[144,3072]{1,0:T(8,128)S(1)} %reshape.195, f32[3072]{0:T(1024)S(1)} %copy-done.5, f32[144]{0:T(256)S(1)} %add_rsqrt_fusion), kind=kOutput, calls=%fused_computation.2 | convolution fusion | flops 7253065728 | bytes 55358016 | tf_op jit(solution)/shard_map/dot_general | solution.py:52
  83.3 0.5 convert_element_type.79
  83.8 0.3 copy.84
  84.1 28.8 %all_to_all.15 = bf16[36,16,768]{2,0,1:T(8,128)(2,1)S(1)} all-to-all(bf16[36,16,768]{2,0,1:T(8,128)(2,1)S(1)} %copy.84), channel_id=1, replica_groups=mesh['dp'=2,'ctx'=4,'tensor'=4] {'ctx','tensor'}, dimensions={1} | all-to-all | bytes 1769472 | tf_op jit(solution)/shard_map/all_to_all | solution.py:134
  112.9 0.2 convert_reduce_fusion
  113.2 1.5 %fusion.15 = bf16[128,768]{1,0:T(8,128)(2,1)} fusion(f32[288,128]{1,0:T(8,128)S(1)} %copy-done.4, f32[288,768]{1,0:T(8,128)S(1)} %reshape.194, f32[128,768]{1,0:T(8,128)S(1)} %copy-done.1, bf16[128,768]{1,0:T(8,128)(2,1)S(1)} %copy-done.3), kind=kOutput, calls=%fused_computation.24 | convolution fusion | flops 340328448 | bytes 1818624 | tf_op jit(solution)/shard_map/dot_general | solution.py:146
  (37 shorter events, 1.6 us)
Async XLA Ops:
  15.2 1.2 %copy-start.6 = (f32[128,2]{0,1:T(2,128)S(1)}, f32[128,2]{0,1:T(2,128)}, u32[]{:S(2)}) copy-start(f32[128,2]{0,1:T(2,128)} %param.23) | copy-start | bytes 3076
  15.2 1.9 %copy-start.2 = (bf16[128,768]{1,0:T(8,128)(2,1)S(1)}, bf16[128,768]{1,0:T(8,128)(2,1)}, u32[]{:S(2)}) copy-start(bf16[128,768]{1,0:T(8,128)(2,1)} %param.17) | copy-start | bytes 589828
  16.3 1.2 %copy-start = (f32[128,768]{1,0:T(8,128)}, f32[128,768]{1,0:T(8,128)S(1)}, u32[]{:S(2)}) copy-start(f32[128,768]{1,0:T(8,128)S(1)} %copy.78) | copy-start | bytes 1179652
  49.2 1.1 copy-start.5
  84.1 29.1 %copy-start.1 = (f32[128,768]{1,0:T(8,128)S(1)}, f32[128,768]{1,0:T(8,128)}, u32[]{:S(2)}) copy-start(f32[128,768]{1,0:T(8,128)} %copy-done) | copy-start | bytes 1179652
  84.1 29.1 %copy-start.3 = (bf16[128,768]{1,0:T(8,128)(2,1)S(1)}, bf16[128,768]{1,0:T(8,128)(2,1)}, u32[]{:S(2)}) copy-start(bf16[128,768]{1,0:T(8,128)(2,1)} %param.17) | copy-start | bytes 589828
  84.1 29.1 %copy-start.4 = (f32[288,128]{1,0:T(8,128)S(1)}, f32[288,128]{1,0:T(8,128)}, u32[]{:S(2)}) copy-start(f32[288,128]{1,0:T(8,128)} %get-tuple-element.6) | copy-start | bytes 442372
where the time goes:
time: 115 us
  blocking collectives  68.4 us (59%)
  matrix products  36.3 us (32%)
  local copies, waits for them, and re-layouts  5.07 us (4%)
  other arithmetic  4.73 us (4%)
    all_to_all x1, blocking collectives, per_device(): lax.all_to_all(outgoing, ('ctx', 'tensor'), split_axis=0, concat_axis=2,...  30.9 us
    all_to_all x1, blocking collectives, per_device(): lax.all_to_all(partial_value.reshape(item_count, n_ctx * n_tensor, quarte...  28.8 us
    dot_general x1, matrix products, expert_block(): return jnp.dot(activated, w_down, preferred_element_type=jnp.float32)  19.5 us
    dot_general x1, matrix products, expert_block(): gate_proj = jnp.dot(normed, w_gate, preferred_element_type=jnp.float32)  13.4 us
    all_gather x1, blocking collectives, per_device(): shard_piece = lax.all_gather(stacked, 'ctx', axis=1, tiled=True)  8.65 us

commit v1 on v0

--- a/solution.py
+++ b/solution.py
@@ -3,6 +3,8 @@
 import jax
 import jax.numpy as jnp
 from jax import lax
+from jax.experimental import pallas as pl
+from jax.experimental.pallas import tpu as pltpu
 from jax.sharding import PartitionSpec as P
 
 HEADS = 24
@@ -153,6 +155,456 @@
     return (hidden_state.astype(jnp.float32) + mixture).astype(jnp.bfloat16)
 
 
+MAIN = 32
+TAIL = 16
+LANES = 256
+BLOCK = 512
+GATE_SLOTS = 5
+DOWN_SLOTS = 3
+MESH = pl.DeviceIdType.MESH
+f32 = jnp.float32
+bf16 = jnp.bfloat16
+
+
+def iota(shape, dim):
+    return lax.broadcasted_iota(jnp.int32, shape, dim)
+
+
+def nt_dot(a, b):
+    return lax.dot_general(a, b, (((1,), (1,)), ((), ())), preferred_element_type=f32)
+
+
+def layer_kernel(
+    n_ctx,
+    n_tensor,
+    q_ref,
+    k_ref,
+    v_ref,
+    ck_ref,
+    cv_ref,
+    res_ref,
+    gain_ref,
+    ids_ref,
+    gw_ref,
+    wg_hbm,
+    wu_hbm,
+    wd_hbm,
+    o_ref,
+    wg_buf,
+    wu_buf,
+    wd_buf,
+    kv_own,
+    kv_buf,
+    hid,
+    msg,
+    got,
+    xs,
+    act,
+    back,
+    landed,
+    pick_main,
+    pick_tail,
+    gate_sem,
+    up_sem,
+    down_sem,
+    kv_send,
+    kv_recv,
+    out_send,
+    out_recv,
+    back_send,
+    back_recv,
+):
+    c = lax.axis_index("ctx")
+    z = lax.axis_index("tensor")
+    me = c * n_tensor + z
+    rows, quarter = res_ref.shape
+    groups = quarter // LANES
+    hidden = wd_hbm.shape[0]
+    n_blocks = hidden // BLOCK
+    per_expert = n_ctx * n_tensor // EXPERTS
+    n_dev = n_ctx * n_tensor
+
+    z_order = (
+        (2, lax.rem(z + 2, 4)),
+        (3, 3 - z),
+        (1, z + 1 - 2 * lax.rem(z, 2)),
+        (0, z),
+    )
+
+    def ctx_at(dc):
+        return lax.rem(c + dc, n_ctx)
+
+    barrier = pltpu.get_barrier_semaphore()
+    for jz, zp in z_order:
+        for dc in range(n_ctx):
+            if jz or dc:
+                pl.semaphore_signal(
+                    barrier,
+                    inc=1,
+                    device_id={"ctx": ctx_at(dc), "tensor": zp},
+                    device_id_type=MESH,
+                )
+    kv_own[0, 0] = ck_ref[...]
+    kv_own[0, 1] = cv_ref[...]
+    kv_own[1, 0] = k_ref[...]
+    kv_own[1, 1] = v_ref[...]
+    pl.semaphore_wait(barrier, n_dev - 1)
+
+    kv_copies = []
+    for dc in range(1, n_ctx):
+        copy = pltpu.make_async_remote_copy(
+            src_ref=kv_own.at[1 - (c + dc) // n_ctx],
+            dst_ref=kv_buf.at[c],
+            send_sem=kv_send.at[dc],
+            recv_sem=kv_recv.at[c],
+            device_id={"ctx": ctx_at(dc), "tensor": z},
+            device_id_type=MESH,
+        )
+        copy.start()
+        kv_copies.append(copy)
+
+    def gate_copy(b):
+        slot = lax.rem(b, GATE_SLOTS)
+        cols = pl.ds(pl.multiple_of(b * BLOCK, BLOCK), BLOCK)
+        return (
+            pltpu.make_async_copy(wg_hbm.at[:, cols], wg_buf.at[slot], gate_sem.at[slot]),
+            pltpu.make_async_copy(wu_hbm.at[:, cols], wu_buf.at[slot], up_sem.at[slot]),
+        )
+
+    def down_copy(step):
+        zp = z_order[step][1]
+        slot = step % DOWN_SLOTS
+        cols = pl.ds(pl.multiple_of(zp * quarter, quarter), quarter)
+        return pltpu.make_async_copy(wd_hbm.at[:, cols], wd_buf.at[slot], down_sem.at[slot])
+
+    for b in range(GATE_SLOTS):
+        for copy in gate_copy(jnp.int32(b)):
+            copy.start()
+    for step in range(DOWN_SLOTS):
+        down_copy(step).start()
+
+    ids = ids_ref[...]
+    id_k = (ids[:, 0:1], ids[:, 1:2])
+    lane = iota((rows, 128), 1)
+    member = ((lane == id_k[0]) | (lane == id_k[1])).astype(f32).astype(bf16)
+    earlier = (iota((rows, rows), 0) > iota((rows, rows), 1)).astype(f32).astype(bf16)
+    count = jnp.dot(earlier, member, preferred_element_type=f32)
+    rank_k = tuple(
+        jnp.sum(jnp.where(lane == e, count, 0.0), axis=1, keepdims=True).astype(jnp.int32)
+        for e in id_k
+    )
+
+    l_main = iota((rows, EXPERTS * MAIN), 1)
+    s_main = jnp.zeros((rows, EXPERTS * MAIN), f32)
+    l_tail = iota((rows, EXPERTS * TAIL), 1)
+    s_tail = jnp.zeros((rows, EXPERTS * TAIL), f32)
+    for k in range(TOP):
+        s_main += (
+            (id_k[k] == l_main // MAIN) & (rank_k[k] == l_main % MAIN)
+        ).astype(f32)
+        s_tail += (
+            (id_k[k] == l_tail // TAIL) & (rank_k[k] == MAIN + l_tail % 4)
+        ).astype(f32)
+    s_main = s_main.T.astype(bf16)
+    s_tails = [
+        jnp.where(l_tail % TAIL // 4 == g, s_tail, 0.0).T.astype(bf16) for g in range(groups)
+    ]
+    p_main = iota((rows, n_dev * MAIN), 1)
+    p_tail = iota((rows, n_dev * TAIL), 1)
+    for k in range(TOP):
+        pick_main[k] = (
+            ((id_k[k] == p_main // (MAIN * per_expert)) & (rank_k[k] == p_main % MAIN))
+            .astype(f32)
+            .astype(bf16)
+        )
+        for g in range(groups):
+            pick_tail[k, g] = (
+                (
+                    (id_k[k] == p_tail // (TAIL * per_expert))
+                    & (rank_k[k] == MAIN + p_tail % 4)
+                    & (p_tail % TAIL // 4 == g)
+                )
+                .astype(f32)
+                .astype(bf16)
+            )
+
+    for dc in range(1, n_ctx):
+        peer = ctx_at(dc)
+        pltpu.make_async_remote_copy(
+            src_ref=kv_own.at[0],
+            dst_ref=kv_buf.at[peer],
+            send_sem=kv_send.at[0],
+            recv_sem=kv_recv.at[peer],
+            device_id={"ctx": peer, "tensor": z},
+            device_id_type=MESH,
+        ).wait_recv()
+    key_rest = jnp.concatenate([kv_buf[ctx_at(dc), 0] for dc in range(1, n_ctx)], axis=0)
+    value_rest = jnp.concatenate([kv_buf[ctx_at(dc), 1] for dc in range(1, n_ctx)], axis=0)
+    seen = iota((rows, rows), 1) <= iota((rows, rows), 0)
+    scale = 1.0 / math.sqrt(HEAD_DIM)
+    for h in range(quarter // HEAD_DIM):
+        cols = slice(h * HEAD_DIM, (h + 1) * HEAD_DIM)
+        head = q_ref[:, cols]
+        s_rest = nt_dot(head, key_rest) * scale
+        s_own = jnp.where(seen, nt_dot(head, k_ref[...]), nt_dot(head, ck_ref[...])) * scale
+        top = jnp.maximum(
+            jnp.max(s_rest, axis=1, keepdims=True), jnp.max(s_own, axis=1, keepdims=True)
+        )
+        w_rest = jnp.exp(s_rest - top)
+        w_own = jnp.exp(s_own - top)
+        total = jnp.sum(w_rest, axis=1, keepdims=True) + jnp.sum(w_own, axis=1, keepdims=True)
+        summed = jnp.dot(w_rest.astype(bf16), value_rest, preferred_element_type=f32)
+        summed += jnp.dot(
+            jnp.where(seen, w_own, 0.0).astype(bf16), v_ref[...], preferred_element_type=f32
+        )
+        summed += jnp.dot(
+            jnp.where(seen, 0.0, w_own).astype(bf16), cv_ref[...], preferred_element_type=f32
+        )
+        hid[:, cols] = (res_ref[:, cols].astype(f32) + summed / total).astype(bf16)
+
+    tails = jnp.zeros((EXPERTS * TAIL, LANES), f32)
+    for g in range(groups):
+        part = hid[:, g * LANES : (g + 1) * LANES]
+        chosen = jnp.dot(s_main, part, preferred_element_type=f32).astype(bf16)
+        msg[:, g * MAIN : (g + 1) * MAIN, :] = chosen.reshape(EXPERTS, MAIN, LANES)
+        tails += jnp.dot(s_tails[g], part, preferred_element_type=f32)
+    msg[:, groups * MAIN :, :] = tails.astype(bf16).reshape(EXPERTS, TAIL, LANES)
+    out_copies = []
+    for jz, zp in z_order:
+        for dc in range(n_ctx):
+            cp = ctx_at(dc)
+            to = (cp * n_tensor + zp) // per_expert
+            if jz or dc:
+                copy = pltpu.make_async_remote_copy(
+                    src_ref=msg.at[to],
+                    dst_ref=got.at[c, z],
+                    send_sem=out_send.at[jz * n_ctx + dc],
+                    recv_sem=out_recv.at[me],
+                    device_id={"ctx": cp, "tensor": zp},
+                    device_id_type=MESH,
+                )
+                copy.start()
+                out_copies.append(copy)
+            else:
+                got[c, z] = msg[to]
+    for jz, zp in z_order[::-1]:
+        for dc in range(n_ctx):
+            if jz or dc:
+                cp = ctx_at(dc)
+                pltpu.make_async_remote_copy(
+                    src_ref=msg.at[0],
+                    dst_ref=got.at[cp, zp],
+                    send_sem=out_send.at[0],
+                    recv_sem=out_recv.at[cp * n_tensor + zp],
+                    device_id={"ctx": cp, "tensor": zp},
+                    device_id_type=MESH,
+                ).wait_recv()
+
+    def normed(full):
+        wide = full.astype(f32)
+        inverse = lax.rsqrt(jnp.mean(wide * wide, axis=1, keepdims=True) + eps)
+        return (wide * inverse * gain_ref[...]).astype(bf16)
+
+    for cp in range(n_ctx):
+        full = jnp.concatenate(
+            [
+                got[cp, q, g * MAIN : (g + 1) * MAIN, :]
+                for q in range(n_tensor)
+                for g in range(groups)
+            ],
+            axis=1,
+        )
+        xs[cp * MAIN : (cp + 1) * MAIN, :] = normed(full)
+    fold_r = iota((n_ctx * 4, n_ctx * TAIL), 0)
+    fold_c = iota((n_ctx * 4, n_ctx * TAIL), 1)
+    fold = [
+        (
+            (fold_r // 4 == fold_c // TAIL)
+            & (fold_r % 4 == fold_c % 4)
+            & (fold_c % TAIL // 4 == g)
+        )
+        .astype(f32)
+        .astype(bf16)
+        for g in range(groups)
+    ]
+    ends = []
+    for q in range(n_tensor):
+        folded = got[:, q, groups * MAIN :, :].reshape(n_ctx * TAIL, LANES)
+        for g in range(groups):
+            ends.append(jnp.dot(fold[g], folded, preferred_element_type=f32))
+    xs[n_ctx * MAIN :, :] = normed(jnp.concatenate(ends, axis=1))
+
+    def gate_block(b, carry):
+        slot = lax.rem(b, GATE_SLOTS)
+        for copy in gate_copy(b):
+            copy.wait()
+        gate = jnp.dot(xs[...], wg_buf[slot], preferred_element_type=f32)
+        up = jnp.dot(xs[...], wu_buf[slot], preferred_element_type=f32)
+        low = (gate / (1.0 + jnp.exp(-gate)) * up).astype(bf16)
+        act[:, pl.ds(pl.multiple_of(b * BLOCK, BLOCK), BLOCK)] = low
+
+        @pl.when(b + GATE_SLOTS < n_blocks)
+        def _():
+            for copy in gate_copy(b + GATE_SLOTS):
+                copy.start()
+
+        return carry
+
+    lax.fori_loop(0, n_blocks, gate_block, 0)
+
+    fold_r = iota((n_ctx * TAIL, n_ctx * 4), 0)
+    fold_c = iota((n_ctx * TAIL, n_ctx * 4), 1)
+    back_copies = []
+    for step, (jz, zp) in enumerate(z_order):
+        down_copy(step).wait()
+        part = jnp.dot(
+            act[...], wd_buf[step % DOWN_SLOTS], preferred_element_type=f32
+        ).astype(bf16)
+        if step + DOWN_SLOTS < n_tensor:
+            down_copy(step + DOWN_SLOTS).start()
+        tails = jnp.zeros((n_ctx * TAIL, LANES), f32)
+        for g in range(groups):
+            cols = slice(g * LANES, (g + 1) * LANES)
+            back[jz, :, g * MAIN : (g + 1) * MAIN, :] = part[: n_ctx * MAIN, cols].reshape(
+                n_ctx, MAIN, LANES
+            )
+            unfold = (
+                (
+                    (fold_c // 4 == fold_r // TAIL)
+                    & (fold_c % 4 == fold_r % 4)
+                    & (fold_r % TAIL // 4 == g)
+                )
+                .astype(f32)
+                .astype(bf16)
+            )
+            tails += jnp.dot(unfold, part[n_ctx * MAIN :, cols], preferred_element_type=f32)
+        back[jz, :, groups * MAIN :, :] = tails.astype(bf16).reshape(n_ctx, TAIL, LANES)
+        for dc in range(n_ctx):
+            cp = ctx_at(dc)
+            if jz or dc:
+                copy = pltpu.make_async_remote_copy(
+                    src_ref=back.at[jz, cp],
+                    dst_ref=landed.at[me],
+                    send_sem=back_send.at[jz * n_ctx + dc],
+                    recv_sem=back_recv.at[me],
+                    device_id={"ctx": cp, "tensor": zp},
+                    device_id_type=MESH,
+                )
+                copy.start()
+                back_copies.append(copy)
+            else:
+                landed[me] = back[jz, cp]
+    for jz, zp in z_order[::-1]:
+        for dc in range(n_ctx):
+            if jz or dc:
+                cp = ctx_at(dc)
+                peer = cp * n_tensor + zp
+                pltpu.make_async_remote_copy(
+                    src_ref=back.at[0, 0],
+                    dst_ref=landed.at[peer],
+                    send_sem=back_send.at[0],
+                    recv_sem=back_recv.at[peer],
+                    device_id={"ctx": cp, "tensor": zp},
+                    device_id_type=MESH,
+                ).wait_recv()
+
+    ends = landed[:, groups * MAIN :, :].reshape(n_dev * TAIL, LANES)
+    for g in range(groups):
+        cols = slice(g * LANES, (g + 1) * LANES)
+        body = landed[:, g * MAIN : (g + 1) * MAIN, :].reshape(n_dev * MAIN, LANES)
+        sums = hid[:, cols].astype(f32)
+        for k in range(TOP):
+            found = jnp.dot(pick_main[k], body, preferred_element_type=f32)
+            found += jnp.dot(pick_tail[k, g], ends, preferred_element_type=f32)
+            sums += gw_ref[:, k : k + 1] * found
+        o_ref[:, cols] = sums.astype(bf16)
+    for copy in kv_copies + out_copies + back_copies:
+        copy.wait_send()
+
+
+def fused(
+    queries,
+    keys,
+    values,
+    cache_keys,
+    cache_values,
+    residual,
+    norm_gain,
+    w_gate,
+    w_up,
+    w_down,
+    expert_ids,
+    gate_weights,
+):
+    n_ctx = lax.axis_size("ctx")
+    n_tensor = lax.axis_size("tensor")
+    rows, quarter = residual.shape
+    width = w_gate.shape[0]
+    hidden = w_gate.shape[1]
+    n_dev = n_ctx * n_tensor
+    length = quarter // LANES * MAIN + TAIL
+    items = n_ctx * CAP
+    vmem = pl.BlockSpec(memory_space=pltpu.VMEM)
+    hbm = pl.BlockSpec(memory_space=pl.ANY)
+    dma = pltpu.SemaphoreType.DMA
+
+    def kernel(*refs):
+        layer_kernel(n_ctx, n_tensor, *refs)
+
+    return pl.pallas_call(
+        kernel,
+        out_shape=jax.ShapeDtypeStruct(residual.shape, bf16),
+        in_specs=[vmem] * 9 + [hbm] * 3,
+        out_specs=vmem,
+        scratch_shapes=[
+            pltpu.VMEM((GATE_SLOTS, width, BLOCK), bf16),
+            pltpu.VMEM((GATE_SLOTS, width, BLOCK), bf16),
+            pltpu.VMEM((DOWN_SLOTS, hidden, quarter), bf16),
+            pltpu.VMEM((2, 2, rows, HEAD_DIM), bf16),
+            pltpu.VMEM((n_ctx, 2, rows, HEAD_DIM), bf16),
+            pltpu.VMEM((rows, quarter), bf16),
+            pltpu.VMEM((EXPERTS, length, LANES), bf16),
+            pltpu.VMEM((n_ctx, n_tensor, length, LANES), bf16),
+            pltpu.VMEM((items, width), bf16),
+            pltpu.VMEM((items, hidden), bf16),
+            pltpu.VMEM((n_tensor, n_ctx, length, LANES), bf16),
+            pltpu.VMEM((n_dev, length, LANES), bf16),
+            pltpu.VMEM((TOP, rows, n_dev * MAIN), bf16),
+            pltpu.VMEM((TOP, quarter // LANES, rows, n_dev * TAIL), bf16),
+            dma((GATE_SLOTS,)),
+            dma((GATE_SLOTS,)),
+            dma((DOWN_SLOTS,)),
+            dma((n_ctx,)),
+            dma((n_ctx,)),
+            dma((n_dev,)),
+            dma((n_dev,)),
+            dma((n_dev,)),
+            dma((n_dev,)),
+        ],
+        compiler_params=pltpu.CompilerParams(
+            collective_id=0, has_side_effects=True, vmem_limit_bytes=60 * 1024 * 1024
+        ),
+        cost_estimate=pl.CostEstimate(
+            flops=6 * items * width * hidden,
+            bytes_accessed=6 * width * hidden,
+            transcendentals=items * hidden,
+        ),
+    )(
+        queries,
+        keys,
+        values,
+        cache_keys,
+        cache_values,
+        residual,
+        norm_gain.reshape(1, width),
+        expert_ids,
+        gate_weights,
+        w_gate,
+        w_up,
+        w_down,
+    )
+
+
 def solution(mesh):
     in_specs = (
         P(("dp", "ctx"), "tensor"),
@@ -169,6 +621,7 @@
         P(("dp", "ctx"), None),
     )
     out_specs = P(("dp", "ctx"), "tensor")
+    fits = mesh.shape["ctx"] == 4 and mesh.shape["tensor"] == 4
     return jax.shard_map(
-        per_device, mesh=mesh, in_specs=in_specs, out_specs=out_specs, check_vma=False
-    )
+        fused if fits else per_device, mesh=mesh, in_specs=in_specs, out_specs=out_specs, check_vma=False
+    )

time: 115 us -> 70.8 us (0.62)
  blocking collectives: 68.4 us -> 0 us
  Pallas kernels: 0 us -> 66.2 us
  matrix products: 36.3 us -> 0 us
  other arithmetic: 4.73 us -> 0 us
    pallas_call x0 -> x1, Pallas kernels: none -> 66.2 us  [fused(): pl.pallas_call(kernel, out_shape=jax.ShapeDtypeStruct(residual.shape, bf1...]
    all_to_all x2 -> x0, blocking collectives: 59.7 us -> none  [the longest x1 30.9 us: per_device(): lax.all_to_all(outgoing, ('ctx', 'tensor'), split_axis=0, concat_axis=2,...]
    dot_general x6 -> x0, matrix products: 36.3 us -> none  [the longest x1 19.5 us: expert_block(): return jnp.dot(activated, w_down, preferred_element_type=jnp.float32)]
    all_gather x1 -> x0, blocking collectives: 8.65 us -> none  [per_device(): shard_piece = lax.all_gather(stacked, 'ctx', axis=1, tiled=True)]
    unnamed x16 -> x3, local copies, waits for them, and re-layouts: 1.91 us -> 4.43 us
    reduce_sum x6 -> x0, other arithmetic: 2.19 us -> none  [the longest x1 0.78 us: route_tables(): jnp.sum(picks.reshape(EXPERTS * CAP, tok_rows, TOP), axis=2)]
    convert_element_type x4 -> x0, local copies, waits for them, and re-layouts: 1.85 us -> none  [the longest x2 1.07 us: expert_block(): widened = full_rows.astype(jnp.float32)]
    another operation x4 -> x0, other arithmetic: 1.46 us -> none  [the longest x1 0.83 us: per_device(): stacked = jnp.stack((cache_keys, cache_values, keys, values))]
where the time goes in v1:
time: 70.8 us; the launch traced here: 70.6 us
  Pallas kernels  66.2 us (94%)
  local copies, waits for them, and re-layouts  4.43 us (6%)
    pallas_call x1, Pallas kernels, fused(): pl.pallas_call(kernel, out_shape=jax.ShapeDtypeStruct(residual.shape, bf1...  66.2 us
    unnamed x3, local copies, waits for them, and re-layouts  4.43 us

profile of v1, /device:TPU:0, one launch (start us, length us, event | category | flops | bytes accessed | tf_op | source)
XLA Modules:
  0.0 70.6 jit_solution(2506082474141186777)
XLA Ops:
  0.0 1.4 %copy.13.refs_7_ = s32[128,2]{1,0:T(8,128)} copy(s32[128,2]{0,1:T(2,128)} %param.22) | data formatting | bytes 2048 | tf_op args[10]
  1.4 1.4 %copy.14.refs_8_ = f32[128,2]{1,0:T(8,128)} copy(f32[128,2]{0,1:T(2,128)} %param.23) | data formatting | bytes 2048 | tf_op args[11]
  2.8 66.2 %shard_map.118 = bf16[128,768]{1,0:T(8,128)(2,1)} custom-call(bf16[128,768]{1,0:T(8,128)(2,1)} %refs_0_.1, bf16[128,128]{1,0:T(8,128)(2,1)} %refs_1_.1, bf16[128,128]{1,0:T(8,128)(2,1)} %refs_2_.1, bf16[128,128]{1,0:T(8,128)(2,1)} %refs_3_.1, bf16[128,128]{1,0:T(8,128)(2,1)} %refs_4_.1, bf16[128,768]{1,0:T(8,128)(2,1)} %refs_5_.1, f32[1,3072]{1,0:T(1,128)} %bitcast.1, ...), custom_call_target="tpu_custom_call" | custom-call | flops 10871635968 | bytes 75497472 | tf_op jit(solution)/shard_map/pallas_call | solution.py:554
  69.0 1.6 %copy.16 = bf16[128,768]{1,0:T(8,128)(2,1)} copy(bf16[128,768]{1,0:T(8,128)(2,1)} %shard_map.118) | data formatting | bytes 393216

commit v2 on v1

--- a/solution.py
+++ b/solution.py
@@ -159,8 +159,8 @@
 TAIL = 16
 LANES = 256
 BLOCK = 512
-GATE_SLOTS = 5
-DOWN_SLOTS = 3
+GATE_SLOTS = 3
+DOWN_SLOTS = 2
 MESH = pl.DeviceIdType.MESH
 f32 = jnp.float32
 bf16 = jnp.bfloat16
@@ -199,6 +199,8 @@
     msg,
     got,
     xs,
+    gate_sum,
+    up_sum,
     act,
     back,
     landed,
@@ -211,6 +213,7 @@
     kv_recv,
     out_send,
     out_recv,
+    pass_send,
     back_send,
     back_recv,
 ):
@@ -230,6 +233,14 @@
         (1, z + 1 - 2 * lax.rem(z, 2)),
         (0, z),
     )
+
+    pair = z // 2
+    mate = z + 1 - 2 * lax.rem(z, 2)
+    near = 2 - pair
+    far = 3 - 3 * pair
+    is_relay = z == 1 + pair
+    end = 3 * pair
+    k_order = (z, mate, near, far)
 
     def ctx_at(dc):
         return lax.rem(c + dc, n_ctx)
@@ -263,12 +274,12 @@
         copy.start()
         kv_copies.append(copy)
 
-    def gate_copy(b):
-        slot = lax.rem(b, GATE_SLOTS)
-        cols = pl.ds(pl.multiple_of(b * BLOCK, BLOCK), BLOCK)
+    def gate_copy(step):
+        slot = step % GATE_SLOTS
+        rows_in = pl.ds(pl.multiple_of(k_order[step] * quarter, quarter), quarter)
         return (
-            pltpu.make_async_copy(wg_hbm.at[:, cols], wg_buf.at[slot], gate_sem.at[slot]),
-            pltpu.make_async_copy(wu_hbm.at[:, cols], wu_buf.at[slot], up_sem.at[slot]),
+            pltpu.make_async_copy(wg_hbm.at[rows_in], wg_buf.at[slot], gate_sem.at[slot]),
+            pltpu.make_async_copy(wu_hbm.at[rows_in], wu_buf.at[slot], up_sem.at[slot]),
         )
 
     def down_copy(step):
@@ -277,8 +288,8 @@
         cols = pl.ds(pl.multiple_of(zp * quarter, quarter), quarter)
         return pltpu.make_async_copy(wd_hbm.at[:, cols], wd_buf.at[slot], down_sem.at[slot])
 
-    for b in range(GATE_SLOTS):
-        for copy in gate_copy(jnp.int32(b)):
+    for step in range(GATE_SLOTS):
+        for copy in gate_copy(step):
             copy.start()
     for step in range(DOWN_SLOTS):
         down_copy(step).start()
@@ -370,15 +381,15 @@
         tails += jnp.dot(s_tails[g], part, preferred_element_type=f32)
     msg[:, groups * MAIN :, :] = tails.astype(bf16).reshape(EXPERTS, TAIL, LANES)
     out_copies = []
-    for jz, zp in z_order:
+    for t, zp in enumerate((near, mate, z)):
         for dc in range(n_ctx):
             cp = ctx_at(dc)
             to = (cp * n_tensor + zp) // per_expert
-            if jz or dc:
+            if t < 2 or dc:
                 copy = pltpu.make_async_remote_copy(
                     src_ref=msg.at[to],
                     dst_ref=got.at[c, z],
-                    send_sem=out_send.at[jz * n_ctx + dc],
+                    send_sem=out_send.at[t * n_ctx + dc],
                     recv_sem=out_recv.at[me],
                     device_id={"ctx": cp, "tensor": zp},
                     device_id_type=MESH,
@@ -387,34 +398,28 @@
                 out_copies.append(copy)
             else:
                 got[c, z] = msg[to]
-    for jz, zp in z_order[::-1]:
-        for dc in range(n_ctx):
-            if jz or dc:
-                cp = ctx_at(dc)
-                pltpu.make_async_remote_copy(
-                    src_ref=msg.at[0],
-                    dst_ref=got.at[cp, zp],
-                    send_sem=out_send.at[0],
-                    recv_sem=out_recv.at[cp * n_tensor + zp],
-                    device_id={"ctx": cp, "tensor": zp},
-                    device_id_type=MESH,
-                ).wait_recv()
-
-    def normed(full):
-        wide = full.astype(f32)
-        inverse = lax.rsqrt(jnp.mean(wide * wide, axis=1, keepdims=True) + eps)
-        return (wide * inverse * gain_ref[...]).astype(bf16)
-
-    for cp in range(n_ctx):
-        full = jnp.concatenate(
-            [
-                got[cp, q, g * MAIN : (g + 1) * MAIN, :]
-                for q in range(n_tensor)
-                for g in range(groups)
-            ],
-            axis=1,
-        )
-        xs[cp * MAIN : (cp + 1) * MAIN, :] = normed(full)
+
+    def arrival(cp, zq):
+        pltpu.make_async_remote_copy(
+            src_ref=msg.at[0],
+            dst_ref=got.at[cp, zq],
+            send_sem=out_send.at[0],
+            recv_sem=out_recv.at[cp * n_tensor + zq],
+            device_id={"ctx": ctx_at(1), "tensor": zq},
+            device_id_type=MESH,
+        ).wait_recv()
+
+    def passing(t, zq, dc):
+        cp = ctx_at(dc)
+        return pltpu.make_async_remote_copy(
+            src_ref=got.at[cp, zq],
+            dst_ref=got.at[cp, zq],
+            send_sem=pass_send.at[t * n_ctx + dc],
+            recv_sem=out_recv.at[cp * n_tensor + zq],
+            device_id={"ctx": c, "tensor": end},
+            device_id_type=MESH,
+        )
+
     fold_r = iota((n_ctx * 4, n_ctx * TAIL), 0)
     fold_c = iota((n_ctx * 4, n_ctx * TAIL), 1)
     fold = [
@@ -427,30 +432,72 @@
         .astype(bf16)
         for g in range(groups)
     ]
-    ends = []
-    for q in range(n_tensor):
-        folded = got[:, q, groups * MAIN :, :].reshape(n_ctx * TAIL, LANES)
-        for g in range(groups):
-            ends.append(jnp.dot(fold[g], folded, preferred_element_type=f32))
-    xs[n_ctx * MAIN :, :] = normed(jnp.concatenate(ends, axis=1))
-
-    def gate_block(b, carry):
-        slot = lax.rem(b, GATE_SLOTS)
-        for copy in gate_copy(b):
+    items = xs.shape[0]
+    squares = jnp.zeros((items, 1), f32)
+    for step, zq in enumerate(k_order):
+        if step < 2:
+            for dc in range(n_ctx):
+                if step or dc:
+                    arrival(ctx_at(dc), zq)
+        else:
+
+            @pl.when(jnp.logical_not(is_relay))
+            def _():
+                for dc in range(n_ctx):
+                    arrival(ctx_at(dc), zq)
+
+        parts = [
+            jnp.concatenate(
+                [got[cp, zq, g * MAIN : (g + 1) * MAIN, :] for g in range(groups)], axis=1
+            ).astype(f32)
+            for cp in range(n_ctx)
+        ]
+        folded = got[:, zq, groups * MAIN :, :].reshape(n_ctx * TAIL, LANES)
+        parts.append(
+            jnp.concatenate(
+                [jnp.dot(fold[g], folded, preferred_element_type=f32) for g in range(groups)],
+                axis=1,
+            )
+        )
+        wide = jnp.concatenate(parts, axis=0)
+        squares += jnp.sum(wide * wide, axis=1, keepdims=True)
+        gain = gain_ref[:, pl.ds(pl.multiple_of(zq * quarter, quarter), quarter)]
+        xs[...] = (wide * gain).astype(bf16)
+        for copy in gate_copy(step):
             copy.wait()
-        gate = jnp.dot(xs[...], wg_buf[slot], preferred_element_type=f32)
-        up = jnp.dot(xs[...], wu_buf[slot], preferred_element_type=f32)
-        low = (gate / (1.0 + jnp.exp(-gate)) * up).astype(bf16)
-        act[:, pl.ds(pl.multiple_of(b * BLOCK, BLOCK), BLOCK)] = low
-
-        @pl.when(b + GATE_SLOTS < n_blocks)
-        def _():
-            for copy in gate_copy(b + GATE_SLOTS):
+        slot = step % GATE_SLOTS
+        last = step == n_tensor - 1
+        if last:
+            inverse = lax.rsqrt(squares / (quarter * n_tensor) + eps)
+
+        def gate_block(b, carry):
+            cols = pl.ds(pl.multiple_of(b * BLOCK, BLOCK), BLOCK)
+            gate = jnp.dot(xs[...], wg_buf[slot, :, cols], preferred_element_type=f32)
+            up = jnp.dot(xs[...], wu_buf[slot, :, cols], preferred_element_type=f32)
+            if step:
+                gate += gate_sum[:, cols]
+                up += up_sum[:, cols]
+            if last:
+                gate *= inverse
+                up *= inverse
+                act[:, cols] = (gate / (1.0 + jnp.exp(-gate)) * up).astype(bf16)
+            else:
+                gate_sum[:, cols] = gate
+                up_sum[:, cols] = up
+            return carry
+
+        lax.fori_loop(0, n_blocks, gate_block, 0)
+        if step + GATE_SLOTS < n_tensor:
+            for copy in gate_copy(step + GATE_SLOTS):
                 copy.start()
-
-        return carry
-
-    lax.fori_loop(0, n_blocks, gate_block, 0)
+        if step == 0:
+
+            @pl.when(is_relay)
+            def _():
+                for t in (0, 1):
+                    for dc in range(n_ctx):
+                        arrival(ctx_at(dc), k_order[2 + t])
+                        passing(t, k_order[2 + t], dc).start()
 
     fold_r = iota((n_ctx * TAIL, n_ctx * 4), 0)
     fold_c = iota((n_ctx * TAIL, n_ctx * 4), 1)
@@ -521,6 +568,12 @@
     for copy in kv_copies + out_copies + back_copies:
         copy.wait_send()
 
+    @pl.when(is_relay)
+    def _():
+        for t in (0, 1):
+            for dc in range(n_ctx):
+                passing(t, k_order[2 + t], dc).wait_send()
+
 
 def fused(
     queries,
@@ -557,15 +610,17 @@
         in_specs=[vmem] * 9 + [hbm] * 3,
         out_specs=vmem,
         scratch_shapes=[
-            pltpu.VMEM((GATE_SLOTS, width, BLOCK), bf16),
-            pltpu.VMEM((GATE_SLOTS, width, BLOCK), bf16),
+            pltpu.VMEM((GATE_SLOTS, quarter, hidden), bf16),
+            pltpu.VMEM((GATE_SLOTS, quarter, hidden), bf16),
             pltpu.VMEM((DOWN_SLOTS, hidden, quarter), bf16),
             pltpu.VMEM((2, 2, rows, HEAD_DIM), bf16),
             pltpu.VMEM((n_ctx, 2, rows, HEAD_DIM), bf16),
             pltpu.VMEM((rows, quarter), bf16),
             pltpu.VMEM((EXPERTS, length, LANES), bf16),
             pltpu.VMEM((n_ctx, n_tensor, length, LANES), bf16),
-            pltpu.VMEM((items, width), bf16),
+            pltpu.VMEM((items, quarter), bf16),
+            pltpu.VMEM((items, hidden), f32),
+            pltpu.VMEM((items, hidden), f32),
             pltpu.VMEM((items, hidden), bf16),
             pltpu.VMEM((n_tensor, n_ctx, length, LANES), bf16),
             pltpu.VMEM((n_dev, length, LANES), bf16),
@@ -578,11 +633,12 @@
             dma((n_ctx,)),
             dma((n_dev,)),
             dma((n_dev,)),
+            dma((2 * n_ctx,)),
             dma((n_dev,)),
             dma((n_dev,)),
         ],
         compiler_params=pltpu.CompilerParams(
-            collective_id=0, has_side_effects=True, vmem_limit_bytes=60 * 1024 * 1024
+            collective_id=0, has_side_effects=True, vmem_limit_bytes=63 * 1024 * 1024
         ),
         cost_estimate=pl.CostEstimate(
             flops=6 * items * width * hidden,

time: 70.8 us -> 65.2 us (0.921)
  the two profiles are of different devices: /device:TPU:0 before, /device:TPU:11 now
where the time goes in v2:
time: 65.2 us; the launch traced here: 65 us
  Pallas kernels  60.5 us (93%)
  local copies, waits for them, and re-layouts  4.43 us (7%)
    pallas_call x1, Pallas kernels, fused(): pl.pallas_call(kernel, out_shape=jax.ShapeDtypeStruct(residual.shape, bf1...  60.5 us
    unnamed x3, local copies, waits for them, and re-layouts  4.43 us

profile of v2, /device:TPU:11, one launch (start us, length us, event | category | flops | bytes accessed | tf_op | source)
XLA Modules:
  0.0 65.0 jit_solution(10968107898624649156)
XLA Ops:
  0.0 1.4 %copy.13.refs_7_ = s32[128,2]{1,0:T(8,128)} copy(s32[128,2]{0,1:T(2,128)} %param.22) | data formatting | bytes 2048 | tf_op args[10]
  1.4 1.4 %copy.14.refs_8_ = f32[128,2]{1,0:T(8,128)} copy(f32[128,2]{0,1:T(2,128)} %param.23) | data formatting | bytes 2048 | tf_op args[11]
  2.8 60.5 %shard_map.118 = bf16[128,768]{1,0:T(8,128)(2,1)} custom-call(bf16[128,768]{1,0:T(8,128)(2,1)} %refs_0_.1, bf16[128,128]{1,0:T(8,128)(2,1)} %refs_1_.1, bf16[128,128]{1,0:T(8,128)(2,1)} %refs_2_.1, bf16[128,128]{1,0:T(8,128)(2,1)} %refs_3_.1, bf16[128,128]{1,0:T(8,128)(2,1)} %refs_4_.1, bf16[128,768]{1,0:T(8,128)(2,1)} %refs_5_.1, f32[1,3072]{1,0:T(1,128)} %bitcast.1, ...), custom_call_target="tpu_custom_call" | custom-call | flops 10871635968 | bytes 75497472 | tf_op jit(solution)/shard_map/pallas_call | solution.py:607
  63.3 1.6 %copy.16 = bf16[128,768]{1,0:T(8,128)(2,1)} copy(bf16[128,768]{1,0:T(8,128)(2,1)} %shard_map.118) | data formatting | bytes 393216
